TPU v7x, 32 devices: a whole 2x2x4 slice. The times are simulated.
32 devices in a mesh: tensor: 4 (over x, core), req: 8 (over z, y).
Axes of the slice: x: 2, y: 2, z: 4, core: 2. Of those that a mesh axis runs over, the one named last changes fastest.
Arguments:
- attention_output: bfloat16 [4096, 4096], P('req', 'tensor'), may hold values from -6 to 6
- residual: bfloat16 [4096, 8192], P('req', 'tensor'), may hold values from -6 to 6
- projection_weight: bfloat16 [4096, 8192], P('tensor'), may hold values from -0.09375 to 0.09375
- adapter_down_maps: bfloat16 [64, 4096, 64], P('req', 'tensor'), may hold values from -0.09375 to 0.09375
- adapter_up_maps: bfloat16 [64, 64, 8192], P('req', None, 'tensor'), may hold values from -0.75 to 0.75
- adapter_pool_slot: int32 [64], replicated, may hold values from 0 to 63, as said below
- request_adapter_id: int32 [8, 8], replicated, may hold values from 0 to 63, as said below
- request_token_length: int32 [8, 8], P('req'), may hold values from 1 to 128, 512 in all within a row
Outputs:
- mixed: bfloat16 [4096, 8192], P('req', 'tensor')
Inputs may be any that keep to these rules, and one draw needn't show every extreme that they name: `adapter_pool_slot`: each slot appears once; the slot s lies on index s // 8 of req, its owner. `request_adapter_id`: the 8 requests of one group use adapters with 8 distinct owners. `request_token_length`: each group's lengths sum to 512; in each group the largest is exactly 128.
All inputs are finite; a program needn't handle non-finite values.
Results may differ from a plain program's by a relative error of at most 0.014.
Values may be sent and summed in bfloat16 or wider, within the bound.
A program may use at most 128 MiB of HBM per device.

v0:
```python
import jax
import jax.numpy as jnp
from jax import lax
from jax.sharding import PartitionSpec as P


def per_device(
    attention_output,
    residual,
    projection_weight,
    adapter_down_maps,
    adapter_up_maps,
    adapter_pool_slot,
    request_adapter_id,
    request_token_length,
):
    groups = lax.axis_size("req")
    me_index = lax.axis_index("req")
    tok_rows = attention_output.shape[0]
    features = attention_output.shape[1]
    pooled_adapter_rows = adapter_down_maps.shape[0]
    lengths = request_token_length[0]
    requests = lengths.shape[0]
    ends = jnp.cumsum(lengths)
    starts = ends - lengths
    my_ids = lax.dynamic_index_in_dim(request_adapter_id, me_index, 0, keepdims=False)
    my_owner = jnp.take(adapter_pool_slot, my_ids) // pooled_adapter_rows
    positions = jnp.arange(tok_rows, dtype=jnp.int32)
    tok_req = jnp.sum((positions[:, None] >= ends[None, :]).astype(jnp.int32), 1)
    req_hot = tok_req[:, None] == jnp.arange(requests, dtype=jnp.int32)[None, :]
    tok_owner = jnp.sum(jnp.where(req_hot, my_owner[None, :], 0), 1)
    tok_start = jnp.sum(jnp.where(req_hot, starts[None, :], 0), 1)
    all_slots = jnp.take(adapter_pool_slot, request_adapter_id)
    mine = all_slots // pooled_adapter_rows == me_index
    block_row_index = jnp.sum(jnp.where(mine, all_slots % pooled_adapter_rows, 0), 1)
    selected_down_map = jnp.take(adapter_down_maps, block_row_index, axis=0)
    selected_up_map = jnp.take(adapter_up_maps, block_row_index, axis=0)
    most_rows = 2 * tok_rows // requests
    owner_hot = my_owner[None, :] == jnp.arange(groups, dtype=jnp.int32)[:, None]
    first = jnp.sum(jnp.where(owner_hot, starts[None, :], 0), 1)
    count = jnp.sum(jnp.where(owner_hot, lengths[None, :], 0), 1)
    slot_pos = jnp.arange(most_rows, dtype=jnp.int32)
    source = first[:, None] + slot_pos[None, :]
    valid = slot_pos[None, :] < count[:, None]
    padded = jnp.concatenate([attention_output, jnp.zeros((1, features), jnp.bfloat16)], 0)
    outgoing = jnp.take(padded, jnp.where(valid, source, tok_rows), axis=0)
    partial_value = jnp.dot(attention_output, projection_weight, preferred_element_type=jnp.float32)
    base = lax.psum_scatter(
        partial_value.astype(jnp.bfloat16), "tensor", scatter_dimension=1, tiled=True
    ).astype(jnp.float32)
    got_down, got_up = (
        lax.all_to_all(selected_down_map, "req", split_axis=0, concat_axis=0, tiled=True),
        lax.all_to_all(selected_up_map, "req", split_axis=0, concat_axis=0, tiled=True),
    )
    reduced_rows = jnp.einsum(
        "sdy,syj->sdj", outgoing, got_down, preferred_element_type=jnp.float32
    )
    reduced_rows = lax.psum(reduced_rows.astype(jnp.bfloat16), "tensor").astype(jnp.float32)
    returned = jnp.einsum(
        "iut,itb->iub",
        reduced_rows.astype(jnp.bfloat16),
        got_up,
        preferred_element_type=jnp.float32,
    )
    flat = returned.reshape(groups * most_rows, returned.shape[2])
    delta = jnp.take(flat, tok_owner * most_rows + positions - tok_start, axis=0)
    return (residual.astype(jnp.float32) + base + delta).astype(jnp.bfloat16)


def solution(mesh):
    in_specs = (
        P("req", "tensor"),
        P("req", "tensor"),
        P("tensor", None),
        P("req", "tensor", None),
        P("req", None, "tensor"),
        P(),
        P(),
        P("req", None),
    )
    out_specs = P("req", "tensor")
    return jax.shard_map(
        per_device, mesh=mesh, in_specs=in_specs, out_specs=out_specs, check_vma=False
    )
```

profile of v0, /device:TPU:15, one launch (start us, length us, event | category | flops | bytes accessed | tf_op | source)
XLA Modules:
  0.0 163.7 jit_solution(6397225064370431403)
XLA Ops:
  6.5 0.0 copy-start
  6.5 0.0 copy-start.1
  6.5 0.9 compare_select_fusion.1
  7.4 0.1 reshape.234
  7.5 0.0 copy-done.1
  7.5 0.0 copy-start.3
  7.5 0.8 gather_fusion.2
  8.3 0.1 reshape.233
  8.4 0.0 copy-done.3
  8.4 0.1 fusion.9
  8.5 1.8 %gather_fusion.3 = bf16[8,1024,64]{1,2,0:T(8,128)(2,1)S(1)} fusion(bf16[8,1024,64]{1,2,0:T(8,128)(2,1)} %param.11, s32[1024]{0:T(1024)S(1)} %pad_clamp_fusion.1), kind=kCustom, calls=%fused_computation.3 | custom fusion | bytes 2097184 | tf_op jit(solution)/shard_map/jit(_take)/gather | solution.py:36
  10.4 0.0 copy-start.4
  10.4 1.2 broadcast_select_fusion.1
  11.6 5.7 %all-to-all-start = ((bf16[8,1024,64]{1,2,0:T(8,128)(2,1)}), bf16[8,1024,64]{1,2,0:T(8,128)(2,1)}, u32[]{:S(2)}, u32[]{:S(2)}) async-start(bf16[8,1024,64]{1,2,0:T(8,128)(2,1)} %broadcast_select_fusion.1), calls=%async_computation.1 | async-start | bytes 2097152 | tf_op jit(solution)/shard_map/all_to_all | solution.py:52
  17.3 0.0 all-reduce.3.cloned.1.call-start
  17.3 0.0 copy-done.4
  17.3 0.2 reduce-window.4
  17.5 0.6 gather_fusion
  18.1 1.3 concatenate.3
  19.4 0.1 select_reduce_fusion.3
  19.6 0.1 fusion.11
  19.7 5.3 %gather_fusion.1 = bf16[1024,1024]{1,0:T(8,128)(2,1)} fusion(bf16[513,1024]{1,0:T(8,128)(2,1)S(1)} %concatenate.3, s32[1024]{0:T(1024)S(1)} %fusion.11), kind=kCustom, calls=%fused_computation.1 | custom fusion | bytes 4198400 | tf_op jit(solution)/shard_map/jit(_take)/gather | solution.py:46
  25.0 0.1 fusion.14
  25.1 15.4 %all-to-all-done = bf16[8,1024,64]{1,2,0:T(8,128)(2,1)} async-done(((bf16[8,1024,64]{1,2,0:T(8,128)(2,1)}), bf16[8,1024,64]{1,2,0:T(8,128)(2,1)}, u32[]{:S(2)}, u32[]{:S(2)}) %all-to-all-start) | async-done | bytes 1048608 | tf_op jit(solution)/shard_map/all_to_all | solution.py:52
  40.4 0.0 copy-start.2
  40.4 3.5 %fusion.3 = bf16[8,128,64]{1,2,0:T(8,128)(2,1)} fusion(bf16[8,1024,64]{1,2,0:T(8,128)(2,1)} %all-to-all-done, bf16[8,128,1024]{2,1,0:T(8,128)(2,1)} %bitcast.38, pred[8,128]{1,0:T(8,128)(4,1)S(1)} %fusion.14), kind=kOutput, calls=%fused_computation.12 | convolution fusion | flops 135331840 | bytes 3277824 | tf_op jit(solution)/shard_map/sdy,syj->sdj/dot_general | solution.py:55
  44.0 0.0 all-reduce.3.cloned.1.call-update
  44.0 0.0 reduce-scatter.2.cloned.1.call-start
  44.0 0.0 copy-done.2
  44.0 16.8 %convolution_convert_fusion = bf16[512,8192]{1,0:T(8,128)(2,1)} fusion(bf16[512,1024]{1,0:T(8,128)(2,1)S(1)} %copy-done.2, bf16[1024,8192]{1,0:T(8,128)(2,1)} %param.10), kind=kOutput, calls=%fused_computation.6 | convolution fusion | flops 8594128896 | bytes 26214400 | tf_op jit(solution)/shard_map/dot_general | solution.py:47
  60.9 0.0 reduce-scatter.2.cloned.1.call-update
  60.9 0.0 copy-done
  60.9 2.0 %gather_fusion.4 = bf16[8,64,2048]{2,1,0:T(8,128)(2,1)} fusion(bf16[8,64,2048]{2,1,0:T(8,128)(2,1)S(1)} %copy-done, s32[1024]{0:T(1024)S(1)} %pad_clamp_fusion.1), kind=kCustom, calls=%fused_computation.4 | custom fusion | bytes 4194336 | tf_op jit(solution)/shard_map/jit(_take)/gather | solution.py:37
  62.9 3.2 %broadcast_select_fusion = bf16[8,64,2048]{2,1,0:T(8,128)(2,1)} fusion(bf16[8,64,2048]{2,1,0:T(8,128)(2,1)} %gather_fusion.4, pred[8]{0:T(512)(128)(4,1)S(1)} %compare_and_fusion), kind=kLoop, calls=%fused_computation.10 | loop fusion | flops 1048576 | bytes 4194312 | tf_op jit(solution)/shard_map/jit(_take)/select_n | solution.py:37
  66.1 6.4 %all-to-all-start.1 = ((bf16[8,64,2048]{2,1,0:T(8,128)(2,1)}), bf16[8,64,2048]{2,1,0:T(8,128)(2,1)}, u32[]{:S(2)}, u32[]{:S(2)}) async-start(bf16[8,64,2048]{2,1,0:T(8,128)(2,1)} %broadcast_select_fusion), calls=%async_computation.2 | async-start | bytes 4194304 | tf_op jit(solution)/shard_map/all_to_all | solution.py:53
  72.5 0.1 convert_reduce_fusion
  72.6 0.1 select_reduce_fusion.1
  72.7 2.8 %all-reduce.3.cloned.1.call-done = bf16[8,128,64]{1,2,0:T(8,128)(2,1)} async-done(((bf16[8,128,64]{1,2,0:T(8,128)(2,1)}), bf16[8,128,64]{1,2,0:T(8,128)(2,1)}) %all-reduce.3.cloned.1.call-update) | async-done | bytes 131088 | tf_op jit(solution)/shard_map/psum | solution.py:58
  75.6 42.6 %all-to-all-done.1 = bf16[8,64,2048]{2,1,0:T(8,128)(2,1)} async-done(((bf16[8,64,2048]{2,1,0:T(8,128)(2,1)}), bf16[8,64,2048]{2,1,0:T(8,128)(2,1)}, u32[]{:S(2)}, u32[]{:S(2)}) %all-to-all-start.1) | async-done | bytes 2097184 | tf_op jit(solution)/shard_map/all_to_all | solution.py:53
  118.2 6.2 %fusion.22 = f32[8,128,2048]{2,1,0:T(8,128)} fusion(bf16[8,128,64]{1,2,0:T(8,128)(2,1)} %all-reduce.3.cloned.1.call-done, bf16[8,64,2048]{2,1,0:T(8,128)(2,1)} %all-to-all-done.1), kind=kOutput, calls=%fused_computation.69 | convolution fusion | flops 268435456 | bytes 10616832 | tf_op jit(solution)/shard_map/iut,itb->iub/dot_general | solution.py:59
  124.4 8.8 %gather_fusion.5 = f32[512,2048]{1,0:T(8,128)} fusion(f32[1024,2048]{1,0:T(8,128)} %bitcast.37, s32[1024]{0:T(1024)S(1)} %pad_clamp_fusion), kind=kCustom, calls=%fused_computation.5 | custom fusion | bytes 8390656 | tf_op jit(solution)/shard_map/jit(_take)/gather | solution.py:66
  133.1 17.8 %reduce-scatter.2.cloned.1.call-done = bf16[512,2048]{1,0:T(8,128)(2,1)} async-done(((bf16[512,8192]{1,0:T(8,128)(2,1)}), bf16[512,2048]{1,0:T(8,128)(2,1)}) %reduce-scatter.2.cloned.1.call-update) | async-done | bytes 2097168 | tf_op jit(solution)/shard_map/reduce_scatter | solution.py:48
  150.9 6.0 %add_convert_fusion = bf16[512,2048]{1,0:T(8,128)(2,1)} fusion(f32[512,2048]{1,0:T(8,128)} %gather_fusion.5, bf16[512,2048]{1,0:T(8,128)(2,1)} %reduce-scatter.2.cloned.1.call-done, bf16[512,2048]{1,0:T(8,128)(2,1)} %param.9, pred[512]{0:T(512)(128)(4,1)S(1)} %compare_and_fusion.1), kind=kLoop, calls=%fused_computation.7 | loop fusion | flops 6291456 | bytes 10486272 | tf_op jit(solution)/shard_map/convert_element_type | solution.py:67
  (12 shorter events, 0.1 us)
Async XLA Ops:
  6.5 54.3 %copy-start = (bf16[8,64,2048]{2,1,0:T(8,128)(2,1)S(1)}, bf16[8,64,2048]{2,1,0:T(8,128)(2,1)}, u32[]{:S(2)}) copy-start(bf16[8,64,2048]{2,1,0:T(8,128)(2,1)} %param.12) | copy-start | bytes 6291460
  6.5 0.9 copy-start.1
  7.5 0.9 copy-start.3
  10.4 6.9 %copy-start.4 = (s32[1,8]{1,0:T(1,128)S(1)}, s32[1,8]{1,0:T(1,128)}, u32[]{:S(2)}) copy-start(s32[1,8]{1,0:T(1,128)} %param.15) | copy-start | bytes 100
  11.6 28.9 %all-to-all-start = ((bf16[8,1024,64]{1,2,0:T(8,128)(2,1)}), bf16[8,1024,64]{1,2,0:T(8,128)(2,1)}, u32[]{:S(2)}, u32[]{:S(2)}) async-start(bf16[8,1024,64]{1,2,0:T(8,128)(2,1)} %broadcast_select_fusion.1), calls=%async_computation.1 | async-start | bytes 2097152 | tf_op jit(solution)/shard_map/all_to_all | solution.py:52
  17.3 58.3 %all-reduce.3.cloned.1.call-start = ((), (), s32[]{:S(2)}) async-start(), calls=%async_computation.4 | async-start | bytes 262144 | tf_op jit(solution)/shard_map/psum | solution.py:58
  40.4 3.6 %copy-start.2 = (bf16[512,1024]{1,0:T(8,128)(2,1)S(1)}, bf16[512,1024]{1,0:T(8,128)(2,1)}, u32[]{:S(2)}) copy-start(bf16[512,1024]{1,0:T(8,128)(2,1)} %param.8) | copy-start | bytes 3145732
  44.0 106.9 %reduce-scatter.2.cloned.1.call-start = ((), (), s32[]{:S(2)}) async-start(), calls=%async_computation.3 | async-start | bytes 10485760 | tf_op jit(solution)/shard_map/reduce_scatter | solution.py:48
  66.1 52.2 %all-to-all-start.1 = ((bf16[8,64,2048]{2,1,0:T(8,128)(2,1)}), bf16[8,64,2048]{2,1,0:T(8,128)(2,1)}, u32[]{:S(2)}, u32[]{:S(2)}) async-start(bf16[8,64,2048]{2,1,0:T(8,128)(2,1)} %broadcast_select_fusion), calls=%async_computation.2 | async-start | bytes 4194304 | tf_op jit(solution)/shard_map/all_to_all | solution.py:53
Sparse Core Ops, SparseCore 0:
  44.1 31.4 all-reduce.2
  78.3 72.5 reduce-scatter.1
where the time goes:
time: 167 us; the launch traced here: 164 us
  waiting for transfers between devices  78.6 us (47%)
  matrix products  26.5 us (16%)
  local copies, waits for them, and re-layouts  20.8 us (12%)
  between operations  13.5 us (8%)
  starting transfers between devices  12.2 us (7%)
  other arithmetic  12.1 us (7%)
    all_to_all x1, waiting for transfers between devices, per_device(): lax.all_to_all(selected_up_map, 'req', split_axis=0, concat_axis=0, tiled...  42.6 us
    reduce_scatter x1, waiting for transfers between devices, per_device(): lax.psum_scatter(partial_value.astype(jnp.bfloat16), 'tensor', scatter_di...  17.8 us
    dot_general x1, matrix products, per_device(): jnp.dot(attention_output, projection_weight, preferred_element_type=jnp.f...  16.8 us
    all_to_all x1, waiting for transfers between devices, per_device(): lax.all_to_all(selected_down_map, 'req', split_axis=0, concat_axis=0, til...  15.4 us
    gather x1, local copies, waits for them, and re-layouts, per_device(): jnp.take(flat, tok_owner * most_rows + positions - tok_start, axis=0)  8.76 us
    all_to_all x1, starting transfers between devices, per_device(): lax.all_to_all(selected_up_map, 'req', split_axis=0, concat_axis=0, tiled...  6.45 us
    dot_general x1, matrix products, per_device(): jnp.einsum('iut,itb->iub', reduced_rows.astype(jnp.bfloat16), got_up, pre...  6.17 us
    convert_element_type x1, other arithmetic, per_device(): return (residual.astype(jnp.float32) + base + delta).astype(jnp.bfloat16)  5.96 us
  transfers between devices with their start and end apart: 4, of which 4 were waited for; matrix products, arithmetic and copies ran while one was open for 27% of the time, Pallas kernels for 0%

commit v1 on v0

v1 whole, which is shorter than its diff:
```python
import functools

import jax
import jax.numpy as jnp
from jax import lax
from jax.experimental import pallas as pl
from jax.experimental.pallas import tpu as pltpu
from jax.sharding import PartitionSpec as P

MESH = pl.DeviceIdType.MESH
BF16 = jnp.bfloat16
F32 = jnp.float32


def select_kernel(rows_ref, down_ref, up_ref, down_out, up_out):
    del rows_ref
    down_out[0] = down_ref[0]
    up_out[0] = up_ref[0]


def select(block_rows, down_maps, up_maps):
    groups = block_rows.shape[0]
    _, rank, depth = down_maps.shape
    width = up_maps.shape[2]
    return pl.pallas_call(
        select_kernel,
        grid_spec=pltpu.PrefetchScalarGridSpec(
            num_scalar_prefetch=1,
            grid=(groups,),
            in_specs=[
                pl.BlockSpec((1, rank, depth), lambda g, rows: (rows[g], 0, 0)),
                pl.BlockSpec((1, rank, width), lambda g, rows: (rows[g], 0, 0)),
            ],
            out_specs=[
                pl.BlockSpec((1, rank, depth), lambda g, rows: (g, 0, 0)),
                pl.BlockSpec((1, rank, width), lambda g, rows: (g, 0, 0)),
            ],
        ),
        out_shape=[
            jax.ShapeDtypeStruct((groups, rank, depth), BF16),
            jax.ShapeDtypeStruct((groups, rank, width), BF16),
        ],
        name="select_adapters",
    )(block_rows, down_maps, up_maps)


def kernel(
    groups, tensor, tile,
    x_ref, w_hbm, res_ref, owner_ref, down_hbm, up_hbm, out_ref,
    w_ref, pair_out, pair_in, chip_out, chip_in, base, down_in, up_in, low_out, low_in, lows,
    w_sem, own_sem, down_send, down_recv, up_send, up_recv,
    pair_send, pair_recv, chip_send, chip_recv, low_send, low_recv,
):
    me_t, me_r = lax.axis_index("tensor"), lax.axis_index("req")
    chips = tensor // 2
    chip, core = me_t // 2, lax.rem(me_t, 2)
    partner = chip * 2 + 1 - core
    width = out_ref.shape[1]
    tiles = width // tile
    rank = up_in.shape[1]
    blocks = []
    for step in range(1, chips + 1):
        there = lax.rem(chip + step, chips)
        blocks += [there * 2 + 1 - core, there * 2 + core]

    def weight_copy(i):
        column = pl.multiple_of(blocks[i] * width, width)
        return pltpu.make_async_copy(w_hbm.at[:, pl.ds(column, width)], w_ref.at[i], w_sem.at[i])

    def down_copy(peer, slot):
        return pltpu.make_async_remote_copy(
            src_ref=down_hbm.at[peer], dst_ref=down_in.at[slot],
            send_sem=down_send.at[peer], recv_sem=down_recv.at[slot],
            device_id=(me_t, peer), device_id_type=MESH)

    def up_copy(peer, slot):
        return pltpu.make_async_remote_copy(
            src_ref=up_hbm.at[peer], dst_ref=up_in.at[slot],
            send_sem=up_send.at[peer], recv_sem=up_recv.at[slot],
            device_id=(me_t, peer), device_id_type=MESH)

    def pair_copy(step, q):
        return pltpu.make_async_remote_copy(
            src_ref=pair_out.at[step, q], dst_ref=pair_in.at[step, q],
            send_sem=pair_send.at[step, q], recv_sem=pair_recv.at[step, q],
            device_id=(partner, me_r), device_id_type=MESH)

    def chip_copy(step, q):
        there = lax.rem(chip + step + 1, chips)
        return pltpu.make_async_remote_copy(
            src_ref=chip_out.at[step, q], dst_ref=chip_in.at[step, q],
            send_sem=chip_send.at[step, q], recv_sem=chip_recv.at[step, q],
            device_id=(there * 2 + core, me_r), device_id_type=MESH)

    def low_copy(step):
        return pltpu.make_async_remote_copy(
            src_ref=low_out, dst_ref=low_in.at[step - 1],
            send_sem=low_send.at[step - 1], recv_sem=low_recv.at[step - 1],
            device_id=(lax.rem(me_t + step, tensor), me_r), device_id_type=MESH)

    for i in range(2 * chips):
        weight_copy(i).start()
    own_down = pltpu.make_async_copy(down_hbm.at[me_r], down_in.at[me_r], own_sem.at[0])
    own_up = pltpu.make_async_copy(up_hbm.at[me_r], up_in.at[me_r], own_sem.at[1])

    barrier = pltpu.get_barrier_semaphore()

    @pl.loop(1, groups)
    def _(d):
        pl.semaphore_signal(
            barrier, inc=1, device_id=(me_t, lax.rem(me_r + d, groups)), device_id_type=MESH)

    for d in range(1, tensor):
        pl.semaphore_signal(
            barrier, inc=1, device_id=(lax.rem(me_t + d, tensor), me_r), device_id_type=MESH)
    pl.semaphore_wait(barrier, groups - 1 + tensor - 1)

    @pl.loop(1, groups)
    def _(d):
        down_copy(lax.rem(me_r + d, groups), me_r).start()

    @pl.loop(1, groups)
    def _(d):
        up_copy(lax.rem(me_r + d, groups), me_r).start()

    own_down.start()
    own_up.start()

    def product(i, q):
        columns = pl.ds(pl.multiple_of(q * tile, tile), tile)
        return jnp.dot(x_ref[...], w_ref[i, :, columns], preferred_element_type=F32)

    for step in range(chips):
        weight_copy(2 * step).wait()

        @pl.loop(0, tiles)
        def _(q):
            pair_out[step, q] = product(2 * step, q).astype(BF16)
            pair_copy(step, q).start()

        weight_copy(2 * step + 1).wait()

        @pl.loop(0, tiles)
        def _(q):
            mine = product(2 * step + 1, q)
            pair_copy(step, q).wait_recv()
            total = mine + pair_in[step, q].astype(F32)
            if step < chips - 1:
                chip_out[step, q] = total.astype(BF16)
                chip_copy(step, q).start()
            else:
                base[q] = total

    own_down.wait()

    @pl.loop(1, groups)
    def _(d):
        peer = lax.rem(me_r + d, groups)
        down_copy(peer, peer).wait_recv()

    span = 2 * rank
    owner = owner_ref[...]
    lane_owner = lax.broadcasted_iota(jnp.int32, (1, span), 1) // rank
    low = jnp.zeros(low_out.shape, F32)
    for pair in range(groups // 2):
        maps = down_in[2 * pair : 2 * pair + 2].reshape(span, x_ref.shape[1])
        value = lax.dot_general(
            x_ref[...], maps, (((1,), (1,)), ((), ())), preferred_element_type=F32)
        low = low + jnp.where(owner == 2 * pair + lane_owner, value, 0.0)
    low_out[...] = low.astype(BF16)
    for step in range(1, tensor):
        low_copy(step).start()
    low = low_out[...].astype(F32)
    for step in range(1, tensor):
        low_copy(step).wait_recv()
        low = low + low_in[step - 1].astype(F32)
    for pair in range(groups // 2):
        lows[:, pair * span : (pair + 1) * span] = jnp.where(
            owner == 2 * pair + lane_owner, low, 0.0).astype(BF16)

    for step in range(chips - 1):
        @pl.loop(0, tiles)
        def _(q):
            chip_copy(step, q).wait_recv()
            base[q] = base[q] + chip_in[step, q].astype(F32)

    own_up.wait()

    @pl.loop(1, groups)
    def _(d):
        peer = lax.rem(me_r + d, groups)
        up_copy(peer, peer).wait_recv()

    @pl.loop(0, tiles)
    def _(q):
        columns = pl.ds(pl.multiple_of(q * tile, tile), tile)
        maps = up_in[:, :, columns].reshape(groups * rank, tile)
        delta = jnp.dot(lows[...], maps, preferred_element_type=F32)
        out_ref[:, columns] = (res_ref[:, columns].astype(F32) + base[q] + delta).astype(BF16)

    @pl.loop(1, groups)
    def _(d):
        peer = lax.rem(me_r + d, groups)
        down_copy(peer, me_r).wait_send()
        up_copy(peer, me_r).wait_send()

    for step in range(chips):
        @pl.loop(0, tiles)
        def _(q):
            pair_copy(step, q).wait_send()
            if step < chips - 1:
                chip_copy(step, q).wait_send()

    for step in range(1, tensor):
        low_copy(step).wait_send()


def per_device(
    attention_output,
    residual,
    projection_weight,
    adapter_down_maps,
    adapter_up_maps,
    adapter_pool_slot,
    request_adapter_id,
    request_token_length,
):
    groups, tensor = lax.axis_size("req"), lax.axis_size("tensor")
    me_index = lax.axis_index("req")
    tokens, depth = attention_output.shape
    width = residual.shape[1]
    pool, _, rank = adapter_down_maps.shape
    lengths = request_token_length[0]
    order = jnp.arange(lengths.shape[0], dtype=jnp.int32)
    ends = jnp.sum(jnp.where(order[None, :] <= order[:, None], lengths[None, :], 0), 1)
    owners = jnp.take(adapter_pool_slot, request_adapter_id) // pool
    slots = jnp.take(adapter_pool_slot, request_adapter_id) % pool
    my_owner = lax.dynamic_index_in_dim(owners, me_index, 0, keepdims=False)
    positions = jnp.arange(tokens, dtype=jnp.int32)
    tok_req = jnp.sum((positions[:, None] >= ends[None, :]).astype(jnp.int32), 1)
    req_hot = tok_req[:, None] == jnp.arange(ends.shape[0], dtype=jnp.int32)[None, :]
    tok_owner = jnp.sum(jnp.where(req_hot, my_owner[None, :], 0), 1, keepdims=True)
    block_rows = jnp.sum(jnp.where(owners == me_index, slots, 0), 1)
    downs, ups = select(block_rows, adapter_down_maps.transpose(0, 2, 1), adapter_up_maps)

    tile = min(512, width)
    tiles = width // tile
    chips = tensor // 2
    far = max(chips - 1, 1)
    vmem = pl.BlockSpec(memory_space=pltpu.VMEM)
    hbm = pl.BlockSpec(memory_space=pl.ANY)
    dma = pltpu.SemaphoreType.DMA
    flops = 2 * tokens * depth * width * tensor
    return pl.pallas_call(
        functools.partial(kernel, groups, tensor, tile),
        out_shape=jax.ShapeDtypeStruct((tokens, width), BF16),
        in_specs=[vmem, hbm, vmem, vmem, hbm, hbm],
        out_specs=vmem,
        scratch_shapes=[
            pltpu.VMEM((tensor, depth, width), BF16),
            pltpu.VMEM((chips, tiles, tokens, tile), BF16),
            pltpu.VMEM((chips, tiles, tokens, tile), BF16),
            pltpu.VMEM((far, tiles, tokens, tile), BF16),
            pltpu.VMEM((far, tiles, tokens, tile), BF16),
            pltpu.VMEM((tiles, tokens, tile), F32),
            pltpu.VMEM((groups, rank, depth), BF16),
            pltpu.VMEM((groups, rank, width), BF16),
            pltpu.VMEM((tokens, 2 * rank), BF16),
            pltpu.VMEM((tensor - 1, tokens, 2 * rank), BF16),
            pltpu.VMEM((tokens, groups * rank), BF16),
            dma((tensor,)),
            dma((2,)),
            dma((groups,)),
            dma((groups,)),
            dma((groups,)),
            dma((groups,)),
            dma((chips, tiles)),
            dma((chips, tiles)),
            dma((far, tiles)),
            dma((far, tiles)),
            dma((tensor - 1,)),
            dma((tensor - 1,)),
        ],
        compiler_params=pltpu.CompilerParams(
            collective_id=0, has_side_effects=True, vmem_limit_bytes=56 * 1024 * 1024
        ),
        cost_estimate=pl.CostEstimate(
            flops=flops, bytes_accessed=2 * depth * width * tensor, transcendentals=0
        ),
        name="project_and_adapt",
    )(attention_output, projection_weight, residual, tok_owner, downs, ups)


def solution(mesh):
    in_specs = (
        P("req", "tensor"),
        P("req", "tensor"),
        P("tensor", None),
        P("req", "tensor", None),
        P("req", None, "tensor"),
        P(),
        P(),
        P("req", None),
    )
    out_specs = P("req", "tensor")
    return jax.shard_map(
        per_device, mesh=mesh, in_specs=in_specs, out_specs=out_specs, check_vma=False
    )
```

time: 167 us -> 92.7 us (0.56); the launches traced: 164 us -> 92.4 us
  Pallas kernels: 0 us -> 85 us
  waiting for transfers between devices: 78.6 us -> 0 us
  matrix products: 26.5 us -> 0 us
  local copies, waits for them, and re-layouts: 20.8 us -> 4.99 us
  between operations: 13.5 us -> 0.03 us
  starting transfers between devices: 12.2 us -> 0 us
  other arithmetic: 12.1 us -> 2.38 us
    pallas_call x0 -> x2, Pallas kernels: none -> 85 us  [the longest x1 78.1 us: per_device(): pl.pallas_call(functools.partial(kernel, groups, tensor, tile), out_shape...]
    all_to_all x2 -> x0, waiting for transfers between devices: 58 us -> none  [the longest x1 42.6 us: per_device(): lax.all_to_all(selected_up_map, 'req', split_axis=0, concat_axis=0, tiled...]
    dot_general x3 -> x0, matrix products: 26.5 us -> none  [the longest x1 16.8 us: per_device(): jnp.dot(attention_output, projection_weight, preferred_element_type=jnp.f...]
    gather x7 -> x2, local copies, waits for them, and re-layouts: 19.4 us -> 0.85 us  [per_device(): owners = jnp.take(adapter_pool_slot, request_adapter_id) // pool]
    reduce_scatter x1 -> x0, waiting for transfers between devices: 17.8 us -> none  [per_device(): lax.psum_scatter(partial_value.astype(jnp.bfloat16), 'tensor', scatter_di...]
    all_to_all x2 -> x0, starting transfers between devices: 12.1 us -> none  [the longest x1 6.45 us: per_device(): lax.all_to_all(selected_up_map, 'req', split_axis=0, concat_axis=0, tiled...]
    convert_element_type x1 -> x0, other arithmetic: 5.96 us -> none  [per_device(): return (residual.astype(jnp.float32) + base + delta).astype(jnp.bfloat16)]
    select_n x6 -> x1, other arithmetic: 5.24 us -> 0.69 us  [per_device(): owners = jnp.take(adapter_pool_slot, request_adapter_id) // pool]
  transfers between devices with their start and end apart: 4 -> 0, of which waited for: 4 -> 0; matrix products, arithmetic and copies ran while one was open for 27% -> 0% of each run, Pallas kernels for 0% -> 0%
where the time goes in v1:
time: 92.7 us; the launch traced here: 92.4 us
  Pallas kernels  85 us (92%)
  local copies, waits for them, and re-layouts  4.99 us (5%)
  other arithmetic  2.38 us (3%)
    pallas_call x1, Pallas kernels, per_device(): pl.pallas_call(functools.partial(kernel, groups, tensor, tile), out_shape...  78.1 us
    pallas_call x1, Pallas kernels, select(): pl.pallas_call(select_kernel, grid_spec=pltpu.PrefetchScalarGridSpec(num_...  6.89 us
    unnamed x5, local copies, waits for them, and re-layouts  3.17 us

profile of v1, /device:TPU:15, one launch (start us, length us, event | category | flops | bytes accessed | tf_op | source)
XLA Modules:
  0.0 92.4 jit_solution(4015043369998563274)
XLA Ops:
  0.0 0.0 copy-start
  0.0 0.8 select_reduce_fusion.1
  0.8 0.1 convert_reduce_fusion
  0.9 0.7 compare_select_fusion
  1.6 0.1 reshape.17
  1.7 0.0 copy-done
  1.7 0.0 copy-start.1
  1.7 0.8 gather_fusion
  2.4 0.1 reshape.20
  2.5 0.0 copy-done.1
  2.5 0.7 fusion.1
  3.3 0.1 select_reduce_fusion
  3.4 0.9 copy.10.owner_ref
  4.2 6.9 %select_adapters.1 = (bf16[8,64,1024]{2,1,0:T(8,128)(2,1)}, bf16[8,64,2048]{2,1,0:T(8,128)(2,1)}) custom-call(s32[8]{0:T(128)} %get-tuple-element.10.rows_ref, bf16[8,64,1024]{2,1,0:T(8,128)(2,1)} %bitcast.5, bf16[8,64,2048]{2,1,0:T(8,128)(2,1)} %up_ref.1), custom_call_target="tpu_custom_call" | custom-call | tf_op jit(solution)/shard_map/select_adapters/pallas_call | solution.py:25
  11.1 78.1 %project_and_adapt.1 = bf16[512,2048]{1,0:T(8,128)(2,1)} custom-call(bf16[512,1024]{1,0:T(8,128)(2,1)} %x_ref.1, bf16[1024,8192]{1,0:T(8,128)(2,1)} %w_hbm.1, bf16[512,2048]{1,0:T(8,128)(2,1)} %res_ref.1, s32[512,1]{1,0:T(8,128)} %copy.10.owner_ref, bf16[8,64,1024]{2,1,0:T(8,128)(2,1)} %get-tuple-element.8.down_hbm, bf16[8,64,2048]{2,1,0:T(8,128)(2,1)} %get-tuple-element.9.up_hbm), custom_call_target="tpu_custom_call" | custom-call | flops 8589934592 | bytes 16777216 | tf_op jit(solution)/shard_map/project_and_adapt/pallas_call | solution.py:254
  89.2 3.2 %copy.12 = bf16[512,2048]{1,0:T(8,128)(2,1)} copy(bf16[512,2048]{1,0:T(8,128)(2,1)} %project_and_adapt.1) | data formatting | bytes 4194304
  (2 shorter events, 0.0 us)
Async XLA Ops:
  0.0 1.7 %copy-start = (s32[64]{0:T(128)S(1)}, s32[64]{0:T(128)}, u32[]{:S(2)}) copy-start(s32[64]{0:T(128)} %param.15) | copy-start | bytes 772
  1.7 0.9 copy-start.1

commit v2 on v1

--- a/solution.py
+++ b/solution.py
@@ -12,50 +12,97 @@
 F32 = jnp.float32
 
 
-def select_kernel(rows_ref, down_ref, up_ref, down_out, up_out):
-    del rows_ref
-    down_out[0] = down_ref[0]
-    up_out[0] = up_ref[0]
-
-
-def select(block_rows, down_maps, up_maps):
-    groups = block_rows.shape[0]
+def select_kernel(
+    slot_ref, id_ref, length_ref, me_ref, down_hbm, up_hbm, down_out, up_out, owner_out, rows, sems
+):
+    groups, requests = id_ref.shape
+    pool = down_hbm.shape[0]
+    me = me_ref[0]
+
+    @pl.loop(0, groups)
+    def _(g):
+        def find(r, row):
+            slot = slot_ref[id_ref[g, r]]
+            return row + jnp.where(slot // pool == me, slot % pool, 0)
+
+        row = lax.fori_loop(0, requests, find, jnp.int32(0), unroll=True)
+        rows[g] = row
+        pltpu.make_async_copy(down_hbm.at[row], down_out.at[g], sems.at[0, g]).start()
+        pltpu.make_async_copy(up_hbm.at[row], up_out.at[g], sems.at[1, g]).start()
+
+    positions = lax.broadcasted_iota(jnp.int32, owner_out.shape, 0)
+    start = jnp.int32(0)
+    owner = jnp.zeros(owner_out.shape, jnp.int32)
+    for r in range(requests):
+        mine = slot_ref[id_ref[me, r]] // pool
+        owner = jnp.where(positions >= start, mine, owner)
+        start = start + length_ref[0, r]
+    owner_out[...] = owner
+
+    @pl.loop(0, groups)
+    def _(g):
+        row = rows[g]
+        pltpu.make_async_copy(down_hbm.at[row], down_out.at[g], sems.at[0, g]).wait()
+        pltpu.make_async_copy(up_hbm.at[row], up_out.at[g], sems.at[1, g]).wait()
+
+
+def select(slots, ids, lengths, me, down_maps, up_maps, tokens):
+    groups = ids.shape[0]
     _, rank, depth = down_maps.shape
     width = up_maps.shape[2]
+    smem = pl.BlockSpec(memory_space=pltpu.SMEM)
+    hbm = pl.BlockSpec(memory_space=pl.ANY)
     return pl.pallas_call(
         select_kernel,
-        grid_spec=pltpu.PrefetchScalarGridSpec(
-            num_scalar_prefetch=1,
-            grid=(groups,),
-            in_specs=[
-                pl.BlockSpec((1, rank, depth), lambda g, rows: (rows[g], 0, 0)),
-                pl.BlockSpec((1, rank, width), lambda g, rows: (rows[g], 0, 0)),
-            ],
-            out_specs=[
-                pl.BlockSpec((1, rank, depth), lambda g, rows: (g, 0, 0)),
-                pl.BlockSpec((1, rank, width), lambda g, rows: (g, 0, 0)),
-            ],
-        ),
+        in_specs=[smem, smem, smem, smem, hbm, hbm],
+        out_specs=[hbm, hbm, pl.BlockSpec(memory_space=pltpu.VMEM)],
         out_shape=[
             jax.ShapeDtypeStruct((groups, rank, depth), BF16),
             jax.ShapeDtypeStruct((groups, rank, width), BF16),
+            jax.ShapeDtypeStruct((tokens, 2 * rank), jnp.int32),
         ],
+        scratch_shapes=[pltpu.SMEM((groups,), jnp.int32), pltpu.SemaphoreType.DMA((2, groups))],
         name="select_adapters",
-    )(block_rows, down_maps, up_maps)
+    )(slots, ids, lengths, me, down_maps, up_maps)
+
+
+def finish_kernel(low_ref, up_ref, base_ref, out_ref):
+    maps = up_ref[...].reshape(low_ref.shape[1], out_ref.shape[1])
+    delta = jnp.dot(low_ref[...], maps, preferred_element_type=F32)
+    out_ref[...] = (base_ref[0] + delta).astype(BF16)
+
+
+def finish(lows, ups, base):
+    tokens, depth = lows.shape
+    groups, rank, width = ups.shape
+    tiles, _, tile = base.shape
+    return pl.pallas_call(
+        finish_kernel,
+        grid=(tiles,),
+        in_specs=[
+            pl.BlockSpec((tokens, depth), lambda q: (0, 0)),
+            pl.BlockSpec((groups, rank, tile), lambda q: (0, 0, q)),
+            pl.BlockSpec((1, tokens, tile), lambda q: (q, 0, 0)),
+        ],
+        out_specs=pl.BlockSpec((tokens, tile), lambda q: (0, q)),
+        out_shape=jax.ShapeDtypeStruct((tokens, width), BF16),
+        compiler_params=pltpu.CompilerParams(vmem_limit_bytes=56 * 1024 * 1024),
+        name="raise_and_add",
+    )(lows, ups, base)
 
 
 def kernel(
     groups, tensor, tile,
-    x_ref, w_hbm, res_ref, owner_ref, down_hbm, up_hbm, out_ref,
-    w_ref, pair_out, pair_in, chip_out, chip_in, base, down_in, up_in, low_out, low_in, lows,
-    w_sem, own_sem, down_send, down_recv, up_send, up_recv,
+    x_ref, w_hbm, res_ref, owner_ref, down_hbm, up_hbm, low_hbm, up_in, base_hbm,
+    w_ref, pair_out, pair_in, chip_out, chip_in, base, down_in, low_out, low_in, lows,
+    w_sem, own_sem, out_sem, down_send, down_recv, up_send, up_recv,
     pair_send, pair_recv, chip_send, chip_recv, low_send, low_recv,
 ):
     me_t, me_r = lax.axis_index("tensor"), lax.axis_index("req")
     chips = tensor // 2
     chip, core = me_t // 2, lax.rem(me_t, 2)
     partner = chip * 2 + 1 - core
-    width = out_ref.shape[1]
+    width = res_ref.shape[1]
     tiles = width // tile
     rank = up_in.shape[1]
     blocks = []
@@ -63,6 +110,10 @@
         there = lax.rem(chip + step, chips)
         blocks += [there * 2 + 1 - core, there * 2 + core]
 
+    def far_first(k):
+        half = (k + 1) // 2
+        return lax.rem(me_r + groups // 2 + half - 2 * half * lax.rem(k, 2), groups)
+
     def weight_copy(i):
         column = pl.multiple_of(blocks[i] * width, width)
         return pltpu.make_async_copy(w_hbm.at[:, pl.ds(column, width)], w_ref.at[i], w_sem.at[i])
@@ -115,13 +166,13 @@
             barrier, inc=1, device_id=(lax.rem(me_t + d, tensor), me_r), device_id_type=MESH)
     pl.semaphore_wait(barrier, groups - 1 + tensor - 1)
 
-    @pl.loop(1, groups)
-    def _(d):
-        down_copy(lax.rem(me_r + d, groups), me_r).start()
-
-    @pl.loop(1, groups)
-    def _(d):
-        up_copy(lax.rem(me_r + d, groups), me_r).start()
+    @pl.loop(0, groups - 1)
+    def _(k):
+        down_copy(far_first(k), me_r).start()
+
+    @pl.loop(0, groups - 1)
+    def _(k):
+        up_copy(far_first(k), me_r).start()
 
     own_down.start()
     own_up.start()
@@ -177,12 +228,21 @@
     for pair in range(groups // 2):
         lows[:, pair * span : (pair + 1) * span] = jnp.where(
             owner == 2 * pair + lane_owner, low, 0.0).astype(BF16)
-
-    for step in range(chips - 1):
-        @pl.loop(0, tiles)
-        def _(q):
+    low_write = pltpu.make_async_copy(lows, low_hbm, own_sem.at[2])
+    low_write.start()
+
+    def base_write(q):
+        return pltpu.make_async_copy(base.at[q], base_hbm.at[q], out_sem.at[q])
+
+    @pl.loop(0, tiles)
+    def _(q):
+        columns = pl.ds(pl.multiple_of(q * tile, tile), tile)
+        total = base[q] + res_ref[:, columns].astype(F32)
+        for step in range(chips - 1):
             chip_copy(step, q).wait_recv()
-            base[q] = base[q] + chip_in[step, q].astype(F32)
+            total = total + chip_in[step, q].astype(F32)
+        base[q] = total
+        base_write(q).start()
 
     own_up.wait()
 
@@ -191,12 +251,11 @@
         peer = lax.rem(me_r + d, groups)
         up_copy(peer, peer).wait_recv()
 
+    low_write.wait()
+
     @pl.loop(0, tiles)
     def _(q):
-        columns = pl.ds(pl.multiple_of(q * tile, tile), tile)
-        maps = up_in[:, :, columns].reshape(groups * rank, tile)
-        delta = jnp.dot(lows[...], maps, preferred_element_type=F32)
-        out_ref[:, columns] = (res_ref[:, columns].astype(F32) + base[q] + delta).astype(BF16)
+        base_write(q).wait()
 
     @pl.loop(1, groups)
     def _(d):
@@ -229,19 +288,11 @@
     me_index = lax.axis_index("req")
     tokens, depth = attention_output.shape
     width = residual.shape[1]
-    pool, _, rank = adapter_down_maps.shape
-    lengths = request_token_length[0]
-    order = jnp.arange(lengths.shape[0], dtype=jnp.int32)
-    ends = jnp.sum(jnp.where(order[None, :] <= order[:, None], lengths[None, :], 0), 1)
-    owners = jnp.take(adapter_pool_slot, request_adapter_id) // pool
-    slots = jnp.take(adapter_pool_slot, request_adapter_id) % pool
-    my_owner = lax.dynamic_index_in_dim(owners, me_index, 0, keepdims=False)
-    positions = jnp.arange(tokens, dtype=jnp.int32)
-    tok_req = jnp.sum((positions[:, None] >= ends[None, :]).astype(jnp.int32), 1)
-    req_hot = tok_req[:, None] == jnp.arange(ends.shape[0], dtype=jnp.int32)[None, :]
-    tok_owner = jnp.sum(jnp.where(req_hot, my_owner[None, :], 0), 1, keepdims=True)
-    block_rows = jnp.sum(jnp.where(owners == me_index, slots, 0), 1)
-    downs, ups = select(block_rows, adapter_down_maps.transpose(0, 2, 1), adapter_up_maps)
+    rank = adapter_down_maps.shape[2]
+    me = jnp.reshape(me_index, (1,))
+    downs, ups, owner = select(
+        adapter_pool_slot, request_adapter_id, request_token_length, me,
+        adapter_down_maps.transpose(0, 2, 1), adapter_up_maps, tokens)
 
     tile = min(512, width)
     tiles = width // tile
@@ -251,11 +302,15 @@
     hbm = pl.BlockSpec(memory_space=pl.ANY)
     dma = pltpu.SemaphoreType.DMA
     flops = 2 * tokens * depth * width * tensor
-    return pl.pallas_call(
+    lows, ups, base = pl.pallas_call(
         functools.partial(kernel, groups, tensor, tile),
-        out_shape=jax.ShapeDtypeStruct((tokens, width), BF16),
+        out_shape=[
+            jax.ShapeDtypeStruct((tokens, groups * rank), BF16),
+            jax.ShapeDtypeStruct((groups, rank, width), BF16),
+            jax.ShapeDtypeStruct((tiles, tokens, tile), F32),
+        ],
         in_specs=[vmem, hbm, vmem, vmem, hbm, hbm],
-        out_specs=vmem,
+        out_specs=[hbm, hbm, hbm],
         scratch_shapes=[
             pltpu.VMEM((tensor, depth, width), BF16),
             pltpu.VMEM((chips, tiles, tokens, tile), BF16),
@@ -264,12 +319,12 @@
             pltpu.VMEM((far, tiles, tokens, tile), BF16),
             pltpu.VMEM((tiles, tokens, tile), F32),
             pltpu.VMEM((groups, rank, depth), BF16),
-            pltpu.VMEM((groups, rank, width), BF16),
             pltpu.VMEM((tokens, 2 * rank), BF16),
             pltpu.VMEM((tensor - 1, tokens, 2 * rank), BF16),
             pltpu.VMEM((tokens, groups * rank), BF16),
             dma((tensor,)),
-            dma((2,)),
+            dma((3,)),
+            dma((tiles,)),
             dma((groups,)),
             dma((groups,)),
             dma((groups,)),
@@ -288,7 +343,8 @@
             flops=flops, bytes_accessed=2 * depth * width * tensor, transcendentals=0
         ),
         name="project_and_adapt",
-    )(attention_output, projection_weight, residual, tok_owner, downs, ups)
+    )(attention_output, projection_weight, residual, owner, downs, ups)
+    return finish(lows, ups, base)
 
 
 def solution(mesh):

time: 92.7 us -> 179 us (1.93)
  Pallas kernels: 85 us -> 179 us
  local copies, waits for them, and re-layouts: 4.99 us -> 0 us
  other arithmetic: 2.38 us -> 0 us
    pallas_call x1 -> x2, Pallas kernels: 6.89 us -> 104 us  [the longest x1 98 us: select(): pl.pallas_call(select_kernel, in_specs=[smem, smem, smem, smem, hbm, hbm]...]
    unnamed x5 -> x0, local copies, waits for them, and re-layouts: 3.17 us -> none
    pallas_call x1, Pallas kernels: 78.1 us -> 75.1 us  [per_device(): pl.pallas_call(functools.partial(kernel, groups, tensor, tile), out_shape...]
where the time goes in v2:
time: 179 us
  Pallas kernels  179 us (100%)
    pallas_call x1, Pallas kernels, select(): pl.pallas_call(select_kernel, in_specs=[smem, smem, smem, smem, hbm, hbm]...  98 us
    pallas_call x1, Pallas kernels, per_device(): pl.pallas_call(functools.partial(kernel, groups, tensor, tile), out_shape...  75.1 us
    pallas_call x1, Pallas kernels, finish(): pl.pallas_call(finish_kernel, grid=(tiles,), in_specs=[pl.BlockSpec((toke...  5.73 us

profile of v2, /device:TPU:15, one launch (start us, length us, event | category | flops | bytes accessed | tf_op | source)
XLA Modules:
  0.0 178.9 jit_solution(8363639909539545005)
XLA Ops:
  0.0 98.0 %select_adapters.1 = (bf16[8,64,1024]{2,1,0:T(8,128)(2,1)}, bf16[8,64,2048]{2,1,0:T(8,128)(2,1)}, s32[512,128]{1,0:T(8,128)}) custom-call(s32[64]{0:T(128)} %slot_ref.1, s32[8,8]{1,0:T(8,128)} %id_ref.1, s32[1,8]{1,0:T(1,128)} %length_ref.1, s32[1]{0:T(128)} %bitcast.me_ref, bf16[8,64,1024]{2,1,0:T(8,128)(2,1)} %bitcast.2, bf16[8,64,2048]{2,1,0:T(8,128)(2,1)} %up_hbm.1), custom_call_target="tpu_custom_call" | custom-call | tf_op jit(solution)/shard_map/select_adapters/pallas_call | solution.py:55
  98.0 75.1 %project_and_adapt.1 = (bf16[512,512]{1,0:T(8,128)(2,1)}, bf16[8,64,2048]{2,1,0:T(8,128)(2,1)}, f32[4,512,512]{2,1,0:T(8,128)}) custom-call(bf16[512,1024]{1,0:T(8,128)(2,1)} %x_ref.1, bf16[1024,8192]{1,0:T(8,128)(2,1)} %w_hbm.1, bf16[512,2048]{1,0:T(8,128)(2,1)} %res_ref.1, s32[512,128]{1,0:T(8,128)} %get-tuple-element.11.owner_ref, ...), custom_call_target="tpu_custom_call" | custom-call | flops 8589934592 | bytes 16777216 | tf_op jit(solution)/shard_map/project_and_adapt/pallas_call | solution.py:305
  173.2 5.7 %raise_and_add.1 = bf16[512,2048]{1,0:T(8,128)(2,1)} custom-call(bf16[512,512]{1,0:T(8,128)(2,1)} %get-tuple-element.14.low_ref, bf16[8,64,2048]{2,1,0:T(8,128)(2,1)} %get-tuple-element.15.up_ref, f32[4,512,512]{2,1,0:T(8,128)} %get-tuple-element.16.base_ref), custom_call_target="tpu_custom_call" | custom-call | tf_op jit(solution)/shard_map/raise_and_add/pallas_call | solution.py:79

commit v3 on v2

--- a/solution.py
+++ b/solution.py
@@ -10,60 +10,6 @@
 MESH = pl.DeviceIdType.MESH
 BF16 = jnp.bfloat16
 F32 = jnp.float32
-
-
-def select_kernel(
-    slot_ref, id_ref, length_ref, me_ref, down_hbm, up_hbm, down_out, up_out, owner_out, rows, sems
-):
-    groups, requests = id_ref.shape
-    pool = down_hbm.shape[0]
-    me = me_ref[0]
-
-    @pl.loop(0, groups)
-    def _(g):
-        def find(r, row):
-            slot = slot_ref[id_ref[g, r]]
-            return row + jnp.where(slot // pool == me, slot % pool, 0)
-
-        row = lax.fori_loop(0, requests, find, jnp.int32(0), unroll=True)
-        rows[g] = row
-        pltpu.make_async_copy(down_hbm.at[row], down_out.at[g], sems.at[0, g]).start()
-        pltpu.make_async_copy(up_hbm.at[row], up_out.at[g], sems.at[1, g]).start()
-
-    positions = lax.broadcasted_iota(jnp.int32, owner_out.shape, 0)
-    start = jnp.int32(0)
-    owner = jnp.zeros(owner_out.shape, jnp.int32)
-    for r in range(requests):
-        mine = slot_ref[id_ref[me, r]] // pool
-        owner = jnp.where(positions >= start, mine, owner)
-        start = start + length_ref[0, r]
-    owner_out[...] = owner
-
-    @pl.loop(0, groups)
-    def _(g):
-        row = rows[g]
-        pltpu.make_async_copy(down_hbm.at[row], down_out.at[g], sems.at[0, g]).wait()
-        pltpu.make_async_copy(up_hbm.at[row], up_out.at[g], sems.at[1, g]).wait()
-
-
-def select(slots, ids, lengths, me, down_maps, up_maps, tokens):
-    groups = ids.shape[0]
-    _, rank, depth = down_maps.shape
-    width = up_maps.shape[2]
-    smem = pl.BlockSpec(memory_space=pltpu.SMEM)
-    hbm = pl.BlockSpec(memory_space=pl.ANY)
-    return pl.pallas_call(
-        select_kernel,
-        in_specs=[smem, smem, smem, smem, hbm, hbm],
-        out_specs=[hbm, hbm, pl.BlockSpec(memory_space=pltpu.VMEM)],
-        out_shape=[
-            jax.ShapeDtypeStruct((groups, rank, depth), BF16),
-            jax.ShapeDtypeStruct((groups, rank, width), BF16),
-            jax.ShapeDtypeStruct((tokens, 2 * rank), jnp.int32),
-        ],
-        scratch_shapes=[pltpu.SMEM((groups,), jnp.int32), pltpu.SemaphoreType.DMA((2, groups))],
-        name="select_adapters",
-    )(slots, ids, lengths, me, down_maps, up_maps)
 
 
 def finish_kernel(low_ref, up_ref, base_ref, out_ref):
@@ -86,16 +32,16 @@
         ],
         out_specs=pl.BlockSpec((tokens, tile), lambda q: (0, q)),
         out_shape=jax.ShapeDtypeStruct((tokens, width), BF16),
-        compiler_params=pltpu.CompilerParams(vmem_limit_bytes=56 * 1024 * 1024),
+        compiler_params=pltpu.CompilerParams(vmem_limit_bytes=60 * 1024 * 1024),
         name="raise_and_add",
     )(lows, ups, base)
 
 
 def kernel(
     groups, tensor, tile,
-    x_ref, w_hbm, res_ref, owner_ref, down_hbm, up_hbm, low_hbm, up_in, base_hbm,
-    w_ref, pair_out, pair_in, chip_out, chip_in, base, down_in, low_out, low_in, lows,
-    w_sem, own_sem, out_sem, down_send, down_recv, up_send, up_recv,
+    slot_ref, id_ref, length_ref, x_ref, w_hbm, res_ref, down_hbm, up_hbm, low_hbm, up_in, base_hbm,
+    w_ref, pair_out, pair_in, chip_out, chip_in, base, down_in, low_out, low_in, lows, down_pool, up_pool, down_out, up_out,
+    w_sem, pool_sem, own_sem, out_sem, down_send, down_recv, up_send, up_recv,
     pair_send, pair_recv, chip_send, chip_recv, low_send, low_recv,
 ):
     me_t, me_r = lax.axis_index("tensor"), lax.axis_index("req")
@@ -120,13 +66,13 @@
 
     def down_copy(peer, slot):
         return pltpu.make_async_remote_copy(
-            src_ref=down_hbm.at[peer], dst_ref=down_in.at[slot],
+            src_ref=down_out.at[peer], dst_ref=down_in.at[slot],
             send_sem=down_send.at[peer], recv_sem=down_recv.at[slot],
             device_id=(me_t, peer), device_id_type=MESH)
 
     def up_copy(peer, slot):
         return pltpu.make_async_remote_copy(
-            src_ref=up_hbm.at[peer], dst_ref=up_in.at[slot],
+            src_ref=up_out.at[peer], dst_ref=up_in.at[slot],
             send_sem=up_send.at[peer], recv_sem=up_recv.at[slot],
             device_id=(me_t, peer), device_id_type=MESH)
 
@@ -149,10 +95,14 @@
             send_sem=low_send.at[step - 1], recv_sem=low_recv.at[step - 1],
             device_id=(lax.rem(me_t + step, tensor), me_r), device_id_type=MESH)
 
+    down_load = pltpu.make_async_copy(down_hbm, down_pool, pool_sem.at[0])
+    up_load = pltpu.make_async_copy(up_hbm, up_pool, pool_sem.at[1])
+    down_load.start()
+    up_load.start()
     for i in range(2 * chips):
         weight_copy(i).start()
-    own_down = pltpu.make_async_copy(down_hbm.at[me_r], down_in.at[me_r], own_sem.at[0])
-    own_up = pltpu.make_async_copy(up_hbm.at[me_r], up_in.at[me_r], own_sem.at[1])
+    own_down = pltpu.make_async_copy(down_out.at[me_r], down_in.at[me_r], own_sem.at[0])
+    own_up = pltpu.make_async_copy(up_out.at[me_r], up_in.at[me_r], own_sem.at[1])
 
     barrier = pltpu.get_barrier_semaphore()
 
@@ -166,14 +116,33 @@
             barrier, inc=1, device_id=(lax.rem(me_t + d, tensor), me_r), device_id_type=MESH)
     pl.semaphore_wait(barrier, groups - 1 + tensor - 1)
 
+    pool, requests = down_pool.shape[0], id_ref.shape[1]
+
+    def wanted(group):
+        row = jnp.int32(0)
+        for r in range(requests):
+            slot = slot_ref[id_ref[group, r]]
+            row = row + jnp.where(slot // pool == me_r, slot % pool, 0)
+        return row
+
+    down_load.wait()
+
     @pl.loop(0, groups - 1)
     def _(k):
-        down_copy(far_first(k), me_r).start()
+        peer = far_first(k)
+        down_out[peer] = down_pool[wanted(peer)]
+        down_copy(peer, me_r).start()
+
+    up_load.wait()
 
     @pl.loop(0, groups - 1)
     def _(k):
-        up_copy(far_first(k), me_r).start()
-
+        peer = far_first(k)
+        up_out[peer] = up_pool[wanted(peer)]
+        up_copy(peer, me_r).start()
+
+    down_out[me_r] = down_pool[wanted(me_r)]
+    up_out[me_r] = up_pool[wanted(me_r)]
     own_down.start()
     own_up.start()
 
@@ -210,7 +179,12 @@
         down_copy(peer, peer).wait_recv()
 
     span = 2 * rank
-    owner = owner_ref[...]
+    positions = lax.broadcasted_iota(jnp.int32, low_out.shape, 0)
+    owner = jnp.zeros(low_out.shape, jnp.int32)
+    start = jnp.int32(0)
+    for r in range(requests):
+        owner = jnp.where(positions >= start, slot_ref[id_ref[me_r, r]] // pool, owner)
+        start = start + length_ref[0, r]
     lane_owner = lax.broadcasted_iota(jnp.int32, (1, span), 1) // rank
     low = jnp.zeros(low_out.shape, F32)
     for pair in range(groups // 2):
@@ -285,19 +259,14 @@
     request_token_length,
 ):
     groups, tensor = lax.axis_size("req"), lax.axis_size("tensor")
-    me_index = lax.axis_index("req")
     tokens, depth = attention_output.shape
     width = residual.shape[1]
-    rank = adapter_down_maps.shape[2]
-    me = jnp.reshape(me_index, (1,))
-    downs, ups, owner = select(
-        adapter_pool_slot, request_adapter_id, request_token_length, me,
-        adapter_down_maps.transpose(0, 2, 1), adapter_up_maps, tokens)
-
+    pool, _, rank = adapter_down_maps.shape
     tile = min(512, width)
     tiles = width // tile
     chips = tensor // 2
     far = max(chips - 1, 1)
+    smem = pl.BlockSpec(memory_space=pltpu.SMEM)
     vmem = pl.BlockSpec(memory_space=pltpu.VMEM)
     hbm = pl.BlockSpec(memory_space=pl.ANY)
     dma = pltpu.SemaphoreType.DMA
@@ -309,7 +278,7 @@
             jax.ShapeDtypeStruct((groups, rank, width), BF16),
             jax.ShapeDtypeStruct((tiles, tokens, tile), F32),
         ],
-        in_specs=[vmem, hbm, vmem, vmem, hbm, hbm],
+        in_specs=[smem, smem, smem, vmem, hbm, vmem, hbm, hbm],
         out_specs=[hbm, hbm, hbm],
         scratch_shapes=[
             pltpu.VMEM((tensor, depth, width), BF16),
@@ -322,7 +291,12 @@
             pltpu.VMEM((tokens, 2 * rank), BF16),
             pltpu.VMEM((tensor - 1, tokens, 2 * rank), BF16),
             pltpu.VMEM((tokens, groups * rank), BF16),
+            pltpu.VMEM((pool, rank, depth), BF16),
+            pltpu.VMEM((pool, rank, width), BF16),
+            pltpu.VMEM((groups, rank, depth), BF16),
+            pltpu.VMEM((groups, rank, width), BF16),
             dma((tensor,)),
+            dma((2,)),
             dma((3,)),
             dma((tiles,)),
             dma((groups,)),
@@ -337,13 +311,17 @@
             dma((tensor - 1,)),
         ],
         compiler_params=pltpu.CompilerParams(
-            collective_id=0, has_side_effects=True, vmem_limit_bytes=56 * 1024 * 1024
+            collective_id=0, has_side_effects=True, vmem_limit_bytes=60 * 1024 * 1024
         ),
         cost_estimate=pl.CostEstimate(
             flops=flops, bytes_accessed=2 * depth * width * tensor, transcendentals=0
         ),
         name="project_and_adapt",
-    )(attention_output, projection_weight, residual, owner, downs, ups)
+    )(
+        adapter_pool_slot, request_adapter_id, request_token_length,
+        attention_output, projection_weight, residual,
+        adapter_down_maps.transpose(0, 2, 1), adapter_up_maps,
+    )
     return finish(lows, ups, base)
 
 

time: 179 us -> 81 us (0.45)
  Pallas kernels: 179 us -> 80.8 us
    pallas_call x1 -> x0, Pallas kernels: 98 us -> none  [select(): pl.pallas_call(select_kernel, in_specs=[smem, smem, smem, smem, hbm, hbm]...]
where the time goes in v3:
time: 81 us; the launch traced here: 80.8 us
  Pallas kernels  80.8 us (100%)
    pallas_call x1, Pallas kernels, per_device(): pl.pallas_call(functools.partial(kernel, groups, tensor, tile), out_shape...  75 us
    pallas_call x1, Pallas kernels, finish(): pl.pallas_call(finish_kernel, grid=(tiles,), in_specs=[pl.BlockSpec((toke...  5.73 us

profile of v3, /device:TPU:15, one launch (start us, length us, event | category | flops | bytes accessed | tf_op | source)
XLA Modules:
  0.0 80.8 jit_solution(6408894601094978856)
XLA Ops:
  0.0 75.0 %project_and_adapt.1 = (bf16[512,512]{1,0:T(8,128)(2,1)}, bf16[8,64,2048]{2,1,0:T(8,128)(2,1)}, f32[4,512,512]{2,1,0:T(8,128)}) custom-call(s32[64]{0:T(128)} %slot_ref.1, s32[8,8]{1,0:T(8,128)} %id_ref.1, s32[1,8]{1,0:T(1,128)} %length_ref.1, bf16[512,1024]{1,0:T(8,128)(2,1)} %x_ref.1, bf16[1024,8192]{1,0:T(8,128)(2,1)} %w_hbm.1, ...), custom_call_target="tpu_custom_call" | custom-call | flops 8589934592 | bytes 16777216 | tf_op jit(solution)/shard_map/project_and_adapt/pallas_call | solution.py:274
  75.0 5.7 %raise_and_add.1 = bf16[512,2048]{1,0:T(8,128)(2,1)} custom-call(bf16[512,512]{1,0:T(8,128)(2,1)} %get-tuple-element.8.low_ref, bf16[8,64,2048]{2,1,0:T(8,128)(2,1)} %get-tuple-element.9.up_ref, f32[4,512,512]{2,1,0:T(8,128)} %get-tuple-element.10.base_ref), custom_call_target="tpu_custom_call" | custom-call | tf_op jit(solution)/shard_map/raise_and_add/pallas_call | solution.py:25
